TPU v7x, 512 devices: a whole 4x8x8 slice. The times are simulated.
512 devices in a mesh: seq: 128 (over z, y, core), tp: 4 (over x).
Axes of the slice: x: 4, y: 8, z: 8, core: 2. Of those that a mesh axis runs over, the one named last changes fastest.
Arguments:
- state: bfloat16 [16384, 1024], P('seq', 'tp'), may hold values from -16 to 16
- cotangent: float32 [16384, 1024], P('seq', 'tp'), may hold values from -40 to 40
- norm_gain: float32 [1024], replicated, may hold values from 0.5 to 1.5
- w_query: bfloat16 [1024, 1024], P(None, 'tp'), may hold values from -8 to 8
- w_key: bfloat16 [1024, 1024], P(None, 'tp'), may hold values from -1 to 1
- w_value: bfloat16 [1024, 1024], P(None, 'tp'), may hold values from -0.1875 to 0.1875
- w_out: bfloat16 [1024, 1024], P('tp'), may hold values from -1.5 to 1.5
Outputs:
- adjoint: float32 [16384, 1024], P('seq', 'tp')
- residual: float32 [16384, 1024], P('seq', 'tp')
All inputs are finite; a program needn't handle non-finite values.
Results may differ from a plain program's by a relative error of at most 0.025.
The roundings to bfloat16 on the way count: a program that leaves them out, or rounds other values in their place, can miss the bound.
Values may be sent and summed in bfloat16 or wider, within the bound.
A program may use at most 64 MiB of HBM per device.

v0:
```python
import math
import jax
import jax.numpy as jnp
from jax import lax
from jax.sharding import Mesh
from jax.sharding import PartitionSpec as P

HD = 128
WIN = 1024
SSTEP = 4
SEQ = ("seq_0", "seq_1", "seq_2")
SEQ_TP = ("seq_0", "seq_1", "seq_2", "tp")
EPSILON = 1e-05


def from_everyone(array, axis):
    copies = jnp.broadcast_to(array, (lax.axis_size(axis), *array.shape))
    return lax.all_to_all(copies, axis, split_axis=0, concat_axis=0, tiled=True)


def in_order(parts, dim):
    dims = list(parts.shape[1:])
    dims[dim] *= parts.shape[0]
    return jnp.moveaxis(parts, 0, dim).reshape(dims)


def collect(array, axis, dim):
    parts = from_everyone(array, axis)
    return in_order(parts, dim)


def shifted(array, axis, by):
    length = lax.axis_size(axis)
    pairs = [(i, i + by) for i in range(length) if 0 <= i + by < length]
    return lax.ppermute(array, axis, pairs)


def cut_along(array, dim, length):
    before, after = (array.shape[:dim], array.shape[dim + 1 :])
    return jnp.moveaxis(array.reshape(*before, length, -1, *after), dim, 0)


def summed_on_arrival(array, axis, dim):
    parts = cut_along(array, dim, lax.axis_size(axis))
    arrived = lax.all_to_all(parts, axis, split_axis=0, concat_axis=0, tiled=True)
    return arrived.sum(axis=0)


def over_axes(array, axes):
    for axis in axes:
        array = lax.psum(array, axis)
    return array


def lower_solve(factor, values):
    result = []
    for index_i in range(values.shape[0]):
        running = values[index_i]
        for index_j in range(index_i):
            running = running - factor[index_i, index_j] * result[index_j]
        result.append(running / factor[index_i, index_i])
    return jnp.stack(result)


def upper_solve(factor, values):
    length_n = values.shape[0]
    result = [None] * length_n
    for index_i in range(length_n - 1, -1, -1):
        running = values[index_i]
        for index_j in range(index_i + 1, length_n):
            running = running - factor[index_j, index_i] * result[index_j]
        result[index_i] = running / factor[index_i, index_i]
    return jnp.stack(result)


def combine_coefficients(gram_matrix, right_side):
    factor = jnp.linalg.cholesky(gram_matrix)
    return upper_solve(factor, lower_solve(factor, right_side))


def on_device(state, cotangent, norm_gain, w_query, w_key, w_value, w_out):
    tok_rows = state.shape[0]
    cols_local = state.shape[1]
    attn_width = w_query.shape[1]
    heads_local = attn_width // HD
    half_span = WIN // 2
    edge_rows = min(tok_rows, half_span)
    reach_count = (half_span + tok_rows - 1) // tok_rows
    key_count = tok_rows + 2 * half_span
    total_rows = tok_rows * lax.axis_size(SEQ)
    first_row = lax.axis_index(SEQ) * tok_rows
    scale_factor = 1.0 / math.sqrt(HD)
    gain_local = lax.dynamic_slice_in_dim(
        norm_gain, lax.axis_index("tp") * cols_local, cols_local, 0
    )
    contract_last = (((1,), (1,)), ((), ()))
    full_state = collect(state, "tp", 1)
    state_full = full_state.astype(jnp.float32)
    inverse = lax.rsqrt(jnp.mean(state_full * state_full, axis=1, keepdims=True) + EPSILON)
    normed = (state_full * inverse * norm_gain[None, :]).astype(jnp.bfloat16)
    w_inputs = jnp.concatenate([w_query, w_key, w_value], axis=1)
    projected = jnp.dot(normed, w_inputs, preferred_element_type=jnp.float32).astype(jnp.bfloat16)
    queries = projected[:, :attn_width].reshape(tok_rows, heads_local, HD)
    key_vecs = projected[:, attn_width : 2 * attn_width].reshape(tok_rows, heads_local, HD)
    values = projected[:, 2 * attn_width :].reshape(tok_rows, heads_local, HD)
    left_parts = []
    for offset in range(reach_count, 0, -1):
        left_parts.append(shifted((key_vecs, values), SEQ, offset))
    right_parts = []
    for offset in range(1, reach_count + 1):
        right_parts.append(shifted((key_vecs, values), SEQ, -offset))
    keys_all = jnp.concatenate(
        [received[0] for received in left_parts]
        + [key_vecs]
        + [received[0] for received in right_parts],
        axis=0,
    )
    values_all = jnp.concatenate(
        [received[1] for received in left_parts]
        + [values]
        + [received[1] for received in right_parts],
        axis=0,
    )
    query_pos = first_row + jnp.arange(tok_rows, dtype=jnp.int32)
    key_pos = first_row - half_span + jnp.arange(key_count, dtype=jnp.int32)
    distance = jnp.abs(key_pos[None, :] - query_pos[:, None])
    valid = ((distance <= half_span) & (key_pos[None, :] >= 0) & (key_pos[None, :] < total_rows))[
        None
    ]
    scores = (
        jnp.einsum("rhe,khe->hrk", queries, keys_all, preferred_element_type=jnp.float32)
        * scale_factor
    )
    row_peak = jnp.max(jnp.where(valid, scores, -jnp.inf), axis=2, keepdims=True)
    raw_weights = jnp.where(valid, jnp.exp(scores - row_peak), 0.0)
    row_total = jnp.sum(raw_weights, axis=2, keepdims=True)
    attn_probs = raw_weights / row_total
    probs_low = attn_probs.astype(jnp.bfloat16)
    attended = jnp.einsum("hrk,khe->rhe", probs_low, values_all, preferred_element_type=jnp.float32)
    krylov = [cotangent]
    differences = []
    for index_n in range(SSTEP):
        whole_vec = collect(krylov[-1].astype(jnp.bfloat16), "tp", 1)
        grad_out = (
            lax.dot_general(whole_vec, w_out, contract_last, preferred_element_type=jnp.float32)
            .astype(jnp.bfloat16)
            .reshape(tok_rows, heads_local, HD)
        )
        row_corr = jnp.sum(grad_out.astype(jnp.float32) * attended, axis=2).T
        grad_prob = jnp.einsum(
            "rhe,khe->hrk", grad_out, values_all, preferred_element_type=jnp.float32
        )
        grad_score = (scale_factor * attn_probs * (grad_prob - row_corr[:, :, None])).astype(
            jnp.bfloat16
        )
        grad_query = jnp.einsum(
            "hrk,khe->rhe", grad_score, keys_all, preferred_element_type=jnp.float32
        ).astype(jnp.bfloat16)
        key_partial = jnp.einsum(
            "hrk,rhe->khe", grad_score, queries, preferred_element_type=jnp.float32
        )
        value_partial = jnp.einsum(
            "hrk,rhe->khe", probs_low, grad_out, preferred_element_type=jnp.float32
        )
        own_key = key_partial[half_span : half_span + tok_rows]
        own_value = value_partial[half_span : half_span + tok_rows]
        for cell_offset in range(1, reach_count + 1):
            lower_row = (reach_count - cell_offset) * edge_rows
            incoming = shifted(
                (
                    key_partial[lower_row : lower_row + edge_rows],
                    value_partial[lower_row : lower_row + edge_rows],
                ),
                SEQ,
                -cell_offset,
            )
            own_key = own_key.at[tok_rows - edge_rows :].add(incoming[0])
            own_value = own_value.at[tok_rows - edge_rows :].add(incoming[1])
        for cell_offset in range(1, reach_count + 1):
            upper_row = half_span + tok_rows + (cell_offset - 1) * edge_rows
            incoming = shifted(
                (
                    key_partial[upper_row : upper_row + edge_rows],
                    value_partial[upper_row : upper_row + edge_rows],
                ),
                SEQ,
                cell_offset,
            )
            own_key = own_key.at[:edge_rows].add(incoming[0])
            own_value = own_value.at[:edge_rows].add(incoming[1])
        grad_key = own_key.astype(jnp.bfloat16)
        grad_value = own_value.astype(jnp.bfloat16)
        stacked = jnp.concatenate(
            [
                grad_query.reshape(tok_rows, attn_width),
                grad_key.reshape(tok_rows, attn_width),
                grad_value.reshape(tok_rows, attn_width),
            ],
            axis=1,
        )
        partial_sum = lax.dot_general(
            stacked, w_inputs, contract_last, preferred_element_type=jnp.float32
        )
        summed = summed_on_arrival(partial_sum, "tp", 1)
        krylov.append(inverse * (gain_local[None, :] * summed))
        differences.append(krylov[index_n] - krylov[index_n + 1])
    diff_stack = jnp.stack(differences)
    local_gram = jnp.einsum("arc,brc->ab", diff_stack, diff_stack, precision=lax.Precision.HIGHEST)
    local_right = jnp.einsum("arc,rc->a", diff_stack, cotangent, precision=lax.Precision.HIGHEST)
    gram_matrix, right_side = (over_axes(local_gram, SEQ_TP), over_axes(local_right, SEQ_TP))
    coefficients = combine_coefficients(gram_matrix, right_side)
    adjoint = coefficients[0] * krylov[0]
    residual = cotangent - coefficients[0] * differences[0]
    for index_n in range(1, SSTEP):
        adjoint = adjoint + coefficients[index_n] * krylov[index_n]
        residual = residual - coefficients[index_n] * differences[index_n]
    return (adjoint, residual)


def solution(mesh):
    split = Mesh(mesh.devices.reshape(8, 8, 2, mesh.shape["tp"]), ("seq_0", "seq_1", "seq_2", "tp"))
    in_specs = (
        P(SEQ, "tp"),
        P(SEQ, "tp"),
        P(),
        P(None, "tp"),
        P(None, "tp"),
        P(None, "tp"),
        P("tp", None),
    )
    out_specs = (P(SEQ, "tp"), P(SEQ, "tp"))
    return jax.shard_map(
        on_device, mesh=split, in_specs=in_specs, out_specs=out_specs, check_vma=False
    )
```

profile of v0, /device:TPU:2, one launch (start us, length us, event | category | flops | bytes accessed | tf_op | source)
XLA Modules:
  0.0 517.0 jit_solution(13610098258207322927)
XLA Ops:
  2.5 9.3 %all-to-all-start = ((bf16[4,128,256]{1,2,0:T(8,128)(2,1)}), bf16[4,128,256]{1,2,0:T(8,128)(2,1)S(1)}, u32[]{:S(2)}, u32[]{:S(2)}) async-start(bf16[4,128,256]{1,2,0:T(8,128)(2,1)} %broadcast_in_dim.28), calls=%async_computation | async-start | bytes 524288 | tf_op jit(solution)/shard_map/all_to_all | solution.py:18
  41.4 7.5 %collective-permute-start.8 = (bf16[128,2,128]{2,0,1:T(8,128)(2,1)}, bf16[128,2,128]{2,0,1:T(8,128)(2,1)S(1)}, u32[]{:S(2)}, u32[]{:S(2)}) collective-permute-start(bf16[128,2,128]{2,0,1:T(8,128)(2,1)} %bitcast.190), channel_id=1, source_target_pairs={{0,16},{4,20},{8,24},{12,28},{16,32},{20,36},{24,40},{28,44},{32,4... | collective-permute-start | bytes 196616 | tf_op jit(solution)/shard_map/ppermute | solution.py:35
  91.2 6.4 %collective-permute-start.22 = (f32[128,2,128]{0,2,1:T(8,128)S(1)}, f32[128,2,128]{0,2,1:T(8,128)S(1)}, u32[]{:S(2)}, u32[]{:S(2)}) collective-permute-start(f32[128,2,128]{0,2,1:T(8,128)S(1)} %get-tuple-element.1346), channel_id=1, source_target_pairs={{0,12},{4,16},{8,20},{12,24},{16,28},{20,32},{24,36},{28,40},{32,4... | collective-permute-start | bytes 393224 | tf_op jit(solution)/shard_map/ppermute | solution.py:35
  97.6 6.2 %collective-permute-start.23 = (f32[128,2,128]{0,2,1:T(8,128)S(1)}, f32[128,2,128]{0,2,1:T(8,128)S(1)}, u32[]{:S(2)}, u32[]{:S(2)}) collective-permute-start(f32[128,2,128]{0,2,1:T(8,128)S(1)} %get-tuple-element.1345), channel_id=1, source_target_pairs={{0,16},{4,20},{8,24},{12,28},{16,32},{20,36},{24,40},{28,44},{32,4... | collective-permute-start | bytes 393224 | tf_op jit(solution)/shard_map/ppermute | solution.py:35
  117.6 7.2 %collective-permute-start.30 = (f32[128,2,128]{0,2,1:T(8,128)S(1)}, f32[128,2,128]{0,2,1:T(8,128)S(1)}, u32[]{:S(2)}, u32[]{:S(2)}) collective-permute-start(f32[128,2,128]{0,2,1:T(8,128)S(1)} %get-tuple-element.1354), channel_id=1, source_target_pairs={{0,12},{4,16},{8,20},{12,24},{16,28},{20,32},{24,36},{28,40},{32,4... | collective-permute-start | bytes 393224 | tf_op jit(solution)/shard_map/ppermute | solution.py:35
  124.8 6.6 %collective-permute-start.31 = (f32[128,2,128]{0,2,1:T(8,128)S(1)}, f32[128,2,128]{0,2,1:T(8,128)S(1)}, u32[]{:S(2)}, u32[]{:S(2)}) collective-permute-start(f32[128,2,128]{0,2,1:T(8,128)S(1)} %get-tuple-element.1353), channel_id=1, source_target_pairs={{0,16},{4,20},{8,24},{12,28},{16,32},{20,36},{24,40},{28,44},{32,4... | collective-permute-start | bytes 393224 | tf_op jit(solution)/shard_map/ppermute | solution.py:35
  143.1 5.5 %all-to-all-done.2 = f32[4,128,256]{2,1,0:T(8,128)} async-done(((f32[4,128,256]{2,1,0:T(8,128)}), f32[4,128,256]{2,1,0:T(8,128)}, u32[]{:S(2)}, u32[]{:S(2)}) %all-to-all-start.2) | async-done | bytes 524320 | tf_op jit(solution)/shard_map/all_to_all | solution.py:45
  153.8 9.1 %all_to_all.45 = bf16[4,128,256]{1,2,0:T(8,128)(2,1)S(1)} all-to-all(bf16[4,128,256]{1,2,0:T(8,128)(2,1)S(1)} %broadcast_in_dim.55), channel_id=1, replica_groups=mesh['seq_0'=8,'seq_1'=8,'seq_2'=2,'tp'=4] {'tp'}, dimensions={0} | all-to-all | bytes 524288 | tf_op jit(solution)/shard_map/all_to_all | solution.py:18
  175.6 8.1 %collective-permute-start.37 = (f32[128,2,128]{0,2,1:T(8,128)S(1)}, f32[128,2,128]{0,2,1:T(8,128)S(1)}, u32[]{:S(2)}, u32[]{:S(2)}) collective-permute-start(f32[128,2,128]{0,2,1:T(8,128)S(1)} %get-tuple-element.1331), channel_id=1, source_target_pairs={{0,8},{4,12},{8,16},{12,20},{16,24},{20,28},{24,32},{28,36},{32,40... | collective-permute-start | bytes 393224 | tf_op jit(solution)/shard_map/ppermute | solution.py:35
  183.9 5.4 %collective-permute-start.38 = (f32[128,2,128]{0,2,1:T(8,128)S(1)}, f32[128,2,128]{0,2,1:T(8,128)S(1)}, u32[]{:S(2)}, u32[]{:S(2)}) collective-permute-start(f32[128,2,128]{0,2,1:T(8,128)S(1)} %get-tuple-element.1330), channel_id=1, source_target_pairs={{0,12},{4,16},{8,20},{12,24},{16,28},{20,32},{24,36},{28,40},{32,4... | collective-permute-start | bytes 393224 | tf_op jit(solution)/shard_map/ppermute | solution.py:35
  189.3 6.1 %collective-permute-start.39 = (f32[128,2,128]{0,2,1:T(8,128)S(1)}, f32[128,2,128]{0,2,1:T(8,128)S(1)}, u32[]{:S(2)}, u32[]{:S(2)}) collective-permute-start(f32[128,2,128]{0,2,1:T(8,128)S(1)} %get-tuple-element.1329), channel_id=1, source_target_pairs={{0,16},{4,20},{8,24},{12,28},{16,32},{20,36},{24,40},{28,44},{32,4... | collective-permute-start | bytes 393224 | tf_op jit(solution)/shard_map/ppermute | solution.py:35
  209.3 7.0 %collective-permute-start.46 = (f32[128,2,128]{0,2,1:T(8,128)S(1)}, f32[128,2,128]{0,2,1:T(8,128)S(1)}, u32[]{:S(2)}, u32[]{:S(2)}) collective-permute-start(f32[128,2,128]{0,2,1:T(8,128)S(1)} %get-tuple-element.1338), channel_id=1, source_target_pairs={{0,12},{4,16},{8,20},{12,24},{16,28},{20,32},{24,36},{28,40},{32,4... | collective-permute-start | bytes 393224 | tf_op jit(solution)/shard_map/ppermute | solution.py:35
  216.4 6.4 %collective-permute-start.47 = (f32[128,2,128]{0,2,1:T(8,128)S(1)}, f32[128,2,128]{0,2,1:T(8,128)S(1)}, u32[]{:S(2)}, u32[]{:S(2)}) collective-permute-start(f32[128,2,128]{0,2,1:T(8,128)S(1)} %get-tuple-element.1337), channel_id=1, source_target_pairs={{0,16},{4,20},{8,24},{12,28},{16,32},{20,36},{24,40},{28,44},{32,4... | collective-permute-start | bytes 393224 | tf_op jit(solution)/shard_map/ppermute | solution.py:35
  227.3 12.2 %all_to_all.46 = f32[4,128,256]{2,1,0:T(8,128)} all-to-all(f32[4,128,256]{2,1,0:T(8,128)S(1)} %bitcast.198), channel_id=1, replica_groups=mesh['seq_0'=8,'seq_1'=8,'seq_2'=2,'tp'=4] {'tp'}, dimensions={0} | all-to-all | bytes 1048576 | tf_op jit(solution)/shard_map/all_to_all | solution.py:45
  243.9 9.1 %all_to_all.47 = bf16[4,128,256]{1,2,0:T(8,128)(2,1)S(1)} all-to-all(bf16[4,128,256]{1,2,0:T(8,128)(2,1)S(1)} %broadcast_in_dim.56), channel_id=1, replica_groups=mesh['seq_0'=8,'seq_1'=8,'seq_2'=2,'tp'=4] {'tp'}, dimensions={0} | all-to-all | bytes 524288 | tf_op jit(solution)/shard_map/all_to_all | solution.py:18
  265.8 7.9 %collective-permute-start.53 = (f32[128,2,128]{0,2,1:T(8,128)S(1)}, f32[128,2,128]{0,2,1:T(8,128)S(1)}, u32[]{:S(2)}, u32[]{:S(2)}) collective-permute-start(f32[128,2,128]{0,2,1:T(8,128)S(1)} %get-tuple-element.1315), channel_id=1, source_target_pairs={{0,8},{4,12},{8,16},{12,20},{16,24},{20,28},{24,32},{28,36},{32,40... | collective-permute-start | bytes 393224 | tf_op jit(solution)/shard_map/ppermute | solution.py:35
  273.8 5.4 %collective-permute-start.54 = (f32[128,2,128]{0,2,1:T(8,128)S(1)}, f32[128,2,128]{0,2,1:T(8,128)S(1)}, u32[]{:S(2)}, u32[]{:S(2)}) collective-permute-start(f32[128,2,128]{0,2,1:T(8,128)S(1)} %get-tuple-element.1314), channel_id=1, source_target_pairs={{0,12},{4,16},{8,20},{12,24},{16,28},{20,32},{24,36},{28,40},{32,4... | collective-permute-start | bytes 393224 | tf_op jit(solution)/shard_map/ppermute | solution.py:35
  279.3 6.1 %collective-permute-start.55 = (f32[128,2,128]{0,2,1:T(8,128)S(1)}, f32[128,2,128]{0,2,1:T(8,128)S(1)}, u32[]{:S(2)}, u32[]{:S(2)}) collective-permute-start(f32[128,2,128]{0,2,1:T(8,128)S(1)} %get-tuple-element.1313), channel_id=1, source_target_pairs={{0,16},{4,20},{8,24},{12,28},{16,32},{20,36},{24,40},{28,44},{32,4... | collective-permute-start | bytes 393224 | tf_op jit(solution)/shard_map/ppermute | solution.py:35
  299.2 7.1 %collective-permute-start.62 = (f32[128,2,128]{0,2,1:T(8,128)S(1)}, f32[128,2,128]{0,2,1:T(8,128)S(1)}, u32[]{:S(2)}, u32[]{:S(2)}) collective-permute-start(f32[128,2,128]{0,2,1:T(8,128)S(1)} %get-tuple-element.1322), channel_id=1, source_target_pairs={{0,12},{4,16},{8,20},{12,24},{16,28},{20,32},{24,36},{28,40},{32,4... | collective-permute-start | bytes 393224 | tf_op jit(solution)/shard_map/ppermute | solution.py:35
  306.3 6.6 %collective-permute-start.63 = (f32[128,2,128]{0,2,1:T(8,128)S(1)}, f32[128,2,128]{0,2,1:T(8,128)S(1)}, u32[]{:S(2)}, u32[]{:S(2)}) collective-permute-start(f32[128,2,128]{0,2,1:T(8,128)S(1)} %get-tuple-element.1321), channel_id=1, source_target_pairs={{0,16},{4,20},{8,24},{12,28},{16,32},{20,36},{24,40},{28,44},{32,4... | collective-permute-start | bytes 393224 | tf_op jit(solution)/shard_map/ppermute | solution.py:35
  316.9 12.3 %all_to_all.48 = f32[4,128,256]{2,1,0:T(8,128)} all-to-all(f32[4,128,256]{2,1,0:T(8,128)S(1)} %bitcast.199), channel_id=1, replica_groups=mesh['seq_0'=8,'seq_1'=8,'seq_2'=2,'tp'=4] {'tp'}, dimensions={0} | all-to-all | bytes 1048576 | tf_op jit(solution)/shard_map/all_to_all | solution.py:45
  333.7 9.1 %all_to_all.49 = bf16[4,128,256]{1,2,0:T(8,128)(2,1)S(1)} all-to-all(bf16[4,128,256]{1,2,0:T(8,128)(2,1)S(1)} %broadcast_in_dim.57), channel_id=1, replica_groups=mesh['seq_0'=8,'seq_1'=8,'seq_2'=2,'tp'=4] {'tp'}, dimensions={0} | all-to-all | bytes 524288 | tf_op jit(solution)/shard_map/all_to_all | solution.py:18
  355.5 8.1 %collective-permute-start.69 = (f32[128,2,128]{0,2,1:T(8,128)S(1)}, f32[128,2,128]{0,2,1:T(8,128)S(1)}, u32[]{:S(2)}, u32[]{:S(2)}) collective-permute-start(f32[128,2,128]{0,2,1:T(8,128)S(1)} %get-tuple-element.1299), channel_id=1, source_target_pairs={{0,8},{4,12},{8,16},{12,20},{16,24},{20,28},{24,32},{28,36},{32,40... | collective-permute-start | bytes 393224 | tf_op jit(solution)/shard_map/ppermute | solution.py:35
  363.8 5.4 %collective-permute-start.70 = (f32[128,2,128]{0,2,1:T(8,128)S(1)}, f32[128,2,128]{0,2,1:T(8,128)S(1)}, u32[]{:S(2)}, u32[]{:S(2)}) collective-permute-start(f32[128,2,128]{0,2,1:T(8,128)S(1)} %get-tuple-element.1298), channel_id=1, source_target_pairs={{0,12},{4,16},{8,20},{12,24},{16,28},{20,32},{24,36},{28,40},{32,4... | collective-permute-start | bytes 393224 | tf_op jit(solution)/shard_map/ppermute | solution.py:35
  369.2 6.1 %collective-permute-start.71 = (f32[128,2,128]{0,2,1:T(8,128)S(1)}, f32[128,2,128]{0,2,1:T(8,128)S(1)}, u32[]{:S(2)}, u32[]{:S(2)}) collective-permute-start(f32[128,2,128]{0,2,1:T(8,128)S(1)} %get-tuple-element.1297), channel_id=1, source_target_pairs={{0,16},{4,20},{8,24},{12,28},{16,32},{20,36},{24,40},{28,44},{32,4... | collective-permute-start | bytes 393224 | tf_op jit(solution)/shard_map/ppermute | solution.py:35
  384.0 5.2 collective-permute-start.77
  389.2 7.2 %collective-permute-start.78 = (f32[128,2,128]{0,2,1:T(8,128)S(1)}, f32[128,2,128]{0,2,1:T(8,128)S(1)}, u32[]{:S(2)}, u32[]{:S(2)}) collective-permute-start(f32[128,2,128]{0,2,1:T(8,128)S(1)} %get-tuple-element.1306), channel_id=1, source_target_pairs={{0,12},{4,16},{8,20},{12,24},{16,28},{20,32},{24,36},{28,40},{32,4... | collective-permute-start | bytes 393224 | tf_op jit(solution)/shard_map/ppermute | solution.py:35
  396.4 6.6 %collective-permute-start.79 = (f32[128,2,128]{0,2,1:T(8,128)S(1)}, f32[128,2,128]{0,2,1:T(8,128)S(1)}, u32[]{:S(2)}, u32[]{:S(2)}) collective-permute-start(f32[128,2,128]{0,2,1:T(8,128)S(1)} %get-tuple-element.1305), channel_id=1, source_target_pairs={{0,16},{4,20},{8,24},{12,28},{16,32},{20,36},{24,40},{28,44},{32,4... | collective-permute-start | bytes 393224 | tf_op jit(solution)/shard_map/ppermute | solution.py:35
  413.0 7.7 %all-to-all-done.8 = f32[4,128,256]{2,1,0:T(8,128)S(1)} async-done(((f32[4,128,256]{2,1,0:T(8,128)}), f32[4,128,256]{2,1,0:T(8,128)S(1)}, u32[]{:S(2)}, u32[]{:S(2)}) %all-to-all-start.8) | async-done | bytes 524320 | tf_op jit(solution)/shard_map/all_to_all | solution.py:45
  426.1 41.4 %all-reduce.1 = (f32[4]{0:T(128)S(1)}, f32[4,4]{0,1:T(4,128)S(1)}) all-reduce(f32[4]{0:T(128)S(1)} %convolution_bitcast_fusion.10, f32[4,4]{0,1:T(4,128)S(1)} %convolution_bitcast_fusion.9), channel_id=1, replica_groups=mesh['seq_0'=8,'seq_1'=8,'seq_2'=2,'tp'=4] {'seq_0'}, use_global_device_ids=true, to_apply=%region_11.12 | all-reduce | flops 20 | bytes 160 | tf_op jit(solution)/shard_map/psum | solution.py:51
  467.5 17.7 %all-reduce = (f32[4]{0:T(128)S(1)}, f32[4,4]{0,1:T(4,128)S(1)}) all-reduce(f32[4]{0:T(128)S(1)} %get-tuple-element.1290, f32[4,4]{0,1:T(4,128)S(1)} %get-tuple-element.1291), channel_id=1, replica_groups=mesh['seq_0'=8,'seq_1'=8,'seq_2'=2,'tp'=4] {'seq_1'}, use_global_device_ids=true, to_apply=%region_12.13 | all-reduce | flops 20 | bytes 160 | tf_op jit(solution)/shard_map/psum | solution.py:51
  487.7 9.2 %all-reduce.2 = (f32[4]{0:T(128)S(1)}, f32[4,4]{0,1:T(4,128)S(1)}) all-reduce(f32[4]{0:T(128)S(1)} %get-tuple-element.1294, f32[4,4]{0,1:T(4,128)S(1)} %get-tuple-element.1295), channel_id=1, replica_groups=mesh['seq_0'=8,'seq_1'=8,'seq_2'=2,'tp'=4] {'tp'}, use_global_device_ids=true, to_apply=%region_14.15 | all-reduce | flops 20 | bytes 160 | tf_op jit(solution)/shard_map/psum | solution.py:51
  (295 shorter events, 217.9 us)
Async XLA Ops:
  37.9 18.8 %collective-permute-start.6 = (bf16[128,2,128]{2,0,1:T(8,128)(2,1)S(1)}, bf16[128,2,128]{2,0,1:T(8,128)(2,1)S(1)}, u32[]{:S(2)}, u32[]{:S(2)}) collective-permute-start(bf16[128,2,128]{2,0,1:T(8,128)(2,1)S(1)} %bitcast.241), channel_id=1, source_target_pairs={{12,0},{16,4},{20,8},{24,12},{28,16},{32,20},{36,24},{40,28},{44,3... | collective-permute-start | bytes 196616 | tf_op jit(solution)/shard_map/ppermute | solution.py:35
  39.2 21.2 %collective-permute-start.7 = (bf16[128,2,128]{2,0,1:T(8,128)(2,1)S(1)}, bf16[128,2,128]{2,0,1:T(8,128)(2,1)S(1)}, u32[]{:S(2)}, u32[]{:S(2)}) collective-permute-start(bf16[128,2,128]{2,0,1:T(8,128)(2,1)S(1)} %bitcast.242), channel_id=1, source_target_pairs={{16,0},{20,4},{24,8},{28,12},{32,16},{36,20},{40,24},{44,28},{48,3... | collective-permute-start | bytes 196616 | tf_op jit(solution)/shard_map/ppermute | solution.py:35
  41.4 21.4 %collective-permute-start.8 = (bf16[128,2,128]{2,0,1:T(8,128)(2,1)}, bf16[128,2,128]{2,0,1:T(8,128)(2,1)S(1)}, u32[]{:S(2)}, u32[]{:S(2)}) collective-permute-start(bf16[128,2,128]{2,0,1:T(8,128)(2,1)} %bitcast.190), channel_id=1, source_target_pairs={{0,16},{4,20},{8,24},{12,28},{16,32},{20,36},{24,40},{28,44},{32,4... | collective-permute-start | bytes 196616 | tf_op jit(solution)/shard_map/ppermute | solution.py:35
  81.7 22.1 %collective-permute-start.19 = (f32[128,2,128]{0,2,1:T(8,128)S(1)}, f32[128,2,128]{0,2,1:T(8,128)S(1)}, u32[]{:S(2)}, u32[]{:S(2)}) collective-permute-start(f32[128,2,128]{0,2,1:T(8,128)S(1)} %get-tuple-element.1349), channel_id=1, source_target_pairs={{16,0},{20,4},{24,8},{28,12},{32,16},{36,20},{40,24},{44,28},{48,3... | collective-permute-start | bytes 393224 | tf_op jit(solution)/shard_map/ppermute | solution.py:35
  83.0 22.1 %collective-permute-start.20 = (f32[128,2,128]{0,2,1:T(8,128)S(1)}, f32[128,2,128]{0,2,1:T(8,128)S(1)}, u32[]{:S(2)}, u32[]{:S(2)}) collective-permute-start(f32[128,2,128]{0,2,1:T(8,128)S(1)} %get-tuple-element.1348), channel_id=1, source_target_pairs={{0,4},{4,8},{8,12},{12,16},{16,20},{20,24},{24,28},{28,32},{32,36}... | collective-permute-start | bytes 393224 | tf_op jit(solution)/shard_map/ppermute | solution.py:35
  86.0 20.3 %collective-permute-start.21 = (f32[128,2,128]{0,2,1:T(8,128)S(1)}, f32[128,2,128]{0,2,1:T(8,128)S(1)}, u32[]{:S(2)}, u32[]{:S(2)}) collective-permute-start(f32[128,2,128]{0,2,1:T(8,128)S(1)} %get-tuple-element.1347), channel_id=1, source_target_pairs={{0,8},{4,12},{8,16},{12,20},{16,24},{20,28},{24,32},{28,36},{32,40... | collective-permute-start | bytes 393224 | tf_op jit(solution)/shard_map/ppermute | solution.py:35
  106.4 18.4 %collective-permute-start.26 = (f32[128,2,128]{0,2,1:T(8,128)S(1)}, f32[128,2,128]{0,2,1:T(8,128)S(1)}, u32[]{:S(2)}, u32[]{:S(2)}) collective-permute-start(f32[128,2,128]{0,2,1:T(8,128)S(1)} %get-tuple-element.1358), channel_id=1, source_target_pairs={{12,0},{16,4},{20,8},{24,12},{28,16},{32,20},{36,24},{40,28},{44,3... | collective-permute-start | bytes 393224 | tf_op jit(solution)/shard_map/ppermute | solution.py:35
  108.1 23.4 %collective-permute-start.27 = (f32[128,2,128]{0,2,1:T(8,128)S(1)}, f32[128,2,128]{0,2,1:T(8,128)S(1)}, u32[]{:S(2)}, u32[]{:S(2)}) collective-permute-start(f32[128,2,128]{0,2,1:T(8,128)S(1)} %get-tuple-element.1357), channel_id=1, source_target_pairs={{16,0},{20,4},{24,8},{28,12},{32,16},{36,20},{40,24},{44,28},{48,3... | collective-permute-start | bytes 393224 | tf_op jit(solution)/shard_map/ppermute | solution.py:35
  109.4 22.1 %collective-permute-start.28 = (f32[128,2,128]{0,2,1:T(8,128)S(1)}, f32[128,2,128]{0,2,1:T(8,128)S(1)}, u32[]{:S(2)}, u32[]{:S(2)}) collective-permute-start(f32[128,2,128]{0,2,1:T(8,128)S(1)} %get-tuple-element.1356), channel_id=1, source_target_pairs={{0,4},{4,8},{8,12},{12,16},{16,20},{20,24},{24,28},{28,32},{32,36}... | collective-permute-start | bytes 393224 | tf_op jit(solution)/shard_map/ppermute | solution.py:35
  112.4 19.0 %collective-permute-start.29 = (f32[128,2,128]{0,2,1:T(8,128)S(1)}, f32[128,2,128]{0,2,1:T(8,128)S(1)}, u32[]{:S(2)}, u32[]{:S(2)}) collective-permute-start(f32[128,2,128]{0,2,1:T(8,128)S(1)} %get-tuple-element.1355), channel_id=1, source_target_pairs={{0,8},{4,12},{8,16},{12,20},{16,24},{20,28},{24,32},{28,36},{32,40... | collective-permute-start | bytes 393224 | tf_op jit(solution)/shard_map/ppermute | solution.py:35
  170.0 19.4 %collective-permute-start.34 = (f32[128,2,128]{0,2,1:T(8,128)S(1)}, f32[128,2,128]{0,2,1:T(8,128)S(1)}, u32[]{:S(2)}, u32[]{:S(2)}) collective-permute-start(f32[128,2,128]{0,2,1:T(8,128)S(1)} %get-tuple-element.1334), channel_id=1, source_target_pairs={{12,0},{16,4},{20,8},{24,12},{28,16},{32,20},{36,24},{40,28},{44,3... | collective-permute-start | bytes 393224 | tf_op jit(solution)/shard_map/ppermute | solution.py:35
  171.3 24.2 %collective-permute-start.35 = (f32[128,2,128]{0,2,1:T(8,128)S(1)}, f32[128,2,128]{0,2,1:T(8,128)S(1)}, u32[]{:S(2)}, u32[]{:S(2)}) collective-permute-start(f32[128,2,128]{0,2,1:T(8,128)S(1)} %get-tuple-element.1333), channel_id=1, source_target_pairs={{16,0},{20,4},{24,8},{28,12},{32,16},{36,20},{40,24},{44,28},{48,3... | collective-permute-start | bytes 393224 | tf_op jit(solution)/shard_map/ppermute | solution.py:35
  172.6 24.2 %collective-permute-start.36 = (f32[128,2,128]{0,2,1:T(8,128)S(1)}, f32[128,2,128]{0,2,1:T(8,128)S(1)}, u32[]{:S(2)}, u32[]{:S(2)}) collective-permute-start(f32[128,2,128]{0,2,1:T(8,128)S(1)} %get-tuple-element.1332), channel_id=1, source_target_pairs={{0,4},{4,8},{8,12},{12,16},{16,20},{20,24},{24,28},{28,32},{32,36}... | collective-permute-start | bytes 393224 | tf_op jit(solution)/shard_map/ppermute | solution.py:35
  175.6 22.5 %collective-permute-start.37 = (f32[128,2,128]{0,2,1:T(8,128)S(1)}, f32[128,2,128]{0,2,1:T(8,128)S(1)}, u32[]{:S(2)}, u32[]{:S(2)}) collective-permute-start(f32[128,2,128]{0,2,1:T(8,128)S(1)} %get-tuple-element.1331), channel_id=1, source_target_pairs={{0,8},{4,12},{8,16},{12,20},{16,24},{20,28},{24,32},{28,36},{32,40... | collective-permute-start | bytes 393224 | tf_op jit(solution)/shard_map/ppermute | solution.py:35
  199.8 23.1 %collective-permute-start.43 = (f32[128,2,128]{0,2,1:T(8,128)S(1)}, f32[128,2,128]{0,2,1:T(8,128)S(1)}, u32[]{:S(2)}, u32[]{:S(2)}) collective-permute-start(f32[128,2,128]{0,2,1:T(8,128)S(1)} %get-tuple-element.1341), channel_id=1, source_target_pairs={{16,0},{20,4},{24,8},{28,12},{32,16},{36,20},{40,24},{44,28},{48,3... | collective-permute-start | bytes 393224 | tf_op jit(solution)/shard_map/ppermute | solution.py:35
  201.1 21.8 %collective-permute-start.44 = (f32[128,2,128]{0,2,1:T(8,128)S(1)}, f32[128,2,128]{0,2,1:T(8,128)S(1)}, u32[]{:S(2)}, u32[]{:S(2)}) collective-permute-start(f32[128,2,128]{0,2,1:T(8,128)S(1)} %get-tuple-element.1340), channel_id=1, source_target_pairs={{0,4},{4,8},{8,12},{12,16},{16,20},{20,24},{24,28},{28,32},{32,36}... | collective-permute-start | bytes 393224 | tf_op jit(solution)/shard_map/ppermute | solution.py:35
  204.2 18.8 %collective-permute-start.45 = (f32[128,2,128]{0,2,1:T(8,128)S(1)}, f32[128,2,128]{0,2,1:T(8,128)S(1)}, u32[]{:S(2)}, u32[]{:S(2)}) collective-permute-start(f32[128,2,128]{0,2,1:T(8,128)S(1)} %get-tuple-element.1339), channel_id=1, source_target_pairs={{0,8},{4,12},{8,16},{12,20},{16,24},{20,28},{24,32},{28,36},{32,40... | collective-permute-start | bytes 393224 | tf_op jit(solution)/shard_map/ppermute | solution.py:35
  260.1 19.2 %collective-permute-start.50 = (f32[128,2,128]{0,2,1:T(8,128)S(1)}, f32[128,2,128]{0,2,1:T(8,128)S(1)}, u32[]{:S(2)}, u32[]{:S(2)}) collective-permute-start(f32[128,2,128]{0,2,1:T(8,128)S(1)} %get-tuple-element.1318), channel_id=1, source_target_pairs={{12,0},{16,4},{20,8},{24,12},{28,16},{32,20},{36,24},{40,28},{44,3... | collective-permute-start | bytes 393224 | tf_op jit(solution)/shard_map/ppermute | solution.py:35
  261.4 24.0 %collective-permute-start.51 = (f32[128,2,128]{0,2,1:T(8,128)S(1)}, f32[128,2,128]{0,2,1:T(8,128)S(1)}, u32[]{:S(2)}, u32[]{:S(2)}) collective-permute-start(f32[128,2,128]{0,2,1:T(8,128)S(1)} %get-tuple-element.1317), channel_id=1, source_target_pairs={{16,0},{20,4},{24,8},{28,12},{32,16},{36,20},{40,24},{44,28},{48,3... | collective-permute-start | bytes 393224 | tf_op jit(solution)/shard_map/ppermute | solution.py:35
  262.7 24.0 %collective-permute-start.52 = (f32[128,2,128]{0,2,1:T(8,128)S(1)}, f32[128,2,128]{0,2,1:T(8,128)S(1)}, u32[]{:S(2)}, u32[]{:S(2)}) collective-permute-start(f32[128,2,128]{0,2,1:T(8,128)S(1)} %get-tuple-element.1316), channel_id=1, source_target_pairs={{0,4},{4,8},{8,12},{12,16},{16,20},{20,24},{24,28},{28,32},{32,36}... | collective-permute-start | bytes 393224 | tf_op jit(solution)/shard_map/ppermute | solution.py:35
  265.8 22.3 %collective-permute-start.53 = (f32[128,2,128]{0,2,1:T(8,128)S(1)}, f32[128,2,128]{0,2,1:T(8,128)S(1)}, u32[]{:S(2)}, u32[]{:S(2)}) collective-permute-start(f32[128,2,128]{0,2,1:T(8,128)S(1)} %get-tuple-element.1315), channel_id=1, source_target_pairs={{0,8},{4,12},{8,16},{12,20},{16,24},{20,28},{24,32},{28,36},{32,40... | collective-permute-start | bytes 393224 | tf_op jit(solution)/shard_map/ppermute | solution.py:35
  289.7 23.3 %collective-permute-start.59 = (f32[128,2,128]{0,2,1:T(8,128)S(1)}, f32[128,2,128]{0,2,1:T(8,128)S(1)}, u32[]{:S(2)}, u32[]{:S(2)}) collective-permute-start(f32[128,2,128]{0,2,1:T(8,128)S(1)} %get-tuple-element.1325), channel_id=1, source_target_pairs={{16,0},{20,4},{24,8},{28,12},{32,16},{36,20},{40,24},{44,28},{48,3... | collective-permute-start | bytes 393224 | tf_op jit(solution)/shard_map/ppermute | solution.py:35
  291.0 22.0 %collective-permute-start.60 = (f32[128,2,128]{0,2,1:T(8,128)S(1)}, f32[128,2,128]{0,2,1:T(8,128)S(1)}, u32[]{:S(2)}, u32[]{:S(2)}) collective-permute-start(f32[128,2,128]{0,2,1:T(8,128)S(1)} %get-tuple-element.1324), channel_id=1, source_target_pairs={{0,4},{4,8},{8,12},{12,16},{16,20},{20,24},{24,28},{28,32},{32,36}... | collective-permute-start | bytes 393224 | tf_op jit(solution)/shard_map/ppermute | solution.py:35
  294.1 18.9 %collective-permute-start.61 = (f32[128,2,128]{0,2,1:T(8,128)S(1)}, f32[128,2,128]{0,2,1:T(8,128)S(1)}, u32[]{:S(2)}, u32[]{:S(2)}) collective-permute-start(f32[128,2,128]{0,2,1:T(8,128)S(1)} %get-tuple-element.1323), channel_id=1, source_target_pairs={{0,8},{4,12},{8,16},{12,20},{16,24},{20,28},{24,32},{28,36},{32,40... | collective-permute-start | bytes 393224 | tf_op jit(solution)/shard_map/ppermute | solution.py:35
  349.8 19.3 %collective-permute-start.66 = (f32[128,2,128]{0,2,1:T(8,128)S(1)}, f32[128,2,128]{0,2,1:T(8,128)S(1)}, u32[]{:S(2)}, u32[]{:S(2)}) collective-permute-start(f32[128,2,128]{0,2,1:T(8,128)S(1)} %get-tuple-element.1302), channel_id=1, source_target_pairs={{12,0},{16,4},{20,8},{24,12},{28,16},{32,20},{36,24},{40,28},{44,3... | collective-permute-start | bytes 393224 | tf_op jit(solution)/shard_map/ppermute | solution.py:35
  351.1 24.2 %collective-permute-start.67 = (f32[128,2,128]{0,2,1:T(8,128)S(1)}, f32[128,2,128]{0,2,1:T(8,128)S(1)}, u32[]{:S(2)}, u32[]{:S(2)}) collective-permute-start(f32[128,2,128]{0,2,1:T(8,128)S(1)} %get-tuple-element.1301), channel_id=1, source_target_pairs={{16,0},{20,4},{24,8},{28,12},{32,16},{36,20},{40,24},{44,28},{48,3... | collective-permute-start | bytes 393224 | tf_op jit(solution)/shard_map/ppermute | solution.py:35
  352.4 24.2 %collective-permute-start.68 = (f32[128,2,128]{0,2,1:T(8,128)S(1)}, f32[128,2,128]{0,2,1:T(8,128)S(1)}, u32[]{:S(2)}, u32[]{:S(2)}) collective-permute-start(f32[128,2,128]{0,2,1:T(8,128)S(1)} %get-tuple-element.1300), channel_id=1, source_target_pairs={{0,4},{4,8},{8,12},{12,16},{16,20},{20,24},{24,28},{28,32},{32,36}... | collective-permute-start | bytes 393224 | tf_op jit(solution)/shard_map/ppermute | solution.py:35
  355.5 22.5 %collective-permute-start.69 = (f32[128,2,128]{0,2,1:T(8,128)S(1)}, f32[128,2,128]{0,2,1:T(8,128)S(1)}, u32[]{:S(2)}, u32[]{:S(2)}) collective-permute-start(f32[128,2,128]{0,2,1:T(8,128)S(1)} %get-tuple-element.1299), channel_id=1, source_target_pairs={{0,8},{4,12},{8,16},{12,20},{16,24},{20,28},{24,32},{28,36},{32,40... | collective-permute-start | bytes 393224 | tf_op jit(solution)/shard_map/ppermute | solution.py:35
  378.0 18.4 %collective-permute-start.74 = (f32[128,2,128]{0,2,1:T(8,128)S(1)}, f32[128,2,128]{0,2,1:T(8,128)S(1)}, u32[]{:S(2)}, u32[]{:S(2)}) collective-permute-start(f32[128,2,128]{0,2,1:T(8,128)S(1)} %get-tuple-element.1310), channel_id=1, source_target_pairs={{12,0},{16,4},{20,8},{24,12},{28,16},{32,20},{36,24},{40,28},{44,3... | collective-permute-start | bytes 393224 | tf_op jit(solution)/shard_map/ppermute | solution.py:35
  379.6 23.4 %collective-permute-start.75 = (f32[128,2,128]{0,2,1:T(8,128)S(1)}, f32[128,2,128]{0,2,1:T(8,128)S(1)}, u32[]{:S(2)}, u32[]{:S(2)}) collective-permute-start(f32[128,2,128]{0,2,1:T(8,128)S(1)} %get-tuple-element.1309), channel_id=1, source_target_pairs={{16,0},{20,4},{24,8},{28,12},{32,16},{36,20},{40,24},{44,28},{48,3... | collective-permute-start | bytes 393224 | tf_op jit(solution)/shard_map/ppermute | solution.py:35
  381.0 22.1 %collective-permute-start.76 = (f32[128,2,128]{0,2,1:T(8,128)S(1)}, f32[128,2,128]{0,2,1:T(8,128)S(1)}, u32[]{:S(2)}, u32[]{:S(2)}) collective-permute-start(f32[128,2,128]{0,2,1:T(8,128)S(1)} %get-tuple-element.1308), channel_id=1, source_target_pairs={{0,4},{4,8},{8,12},{12,16},{16,20},{20,24},{24,28},{28,32},{32,36}... | collective-permute-start | bytes 393224 | tf_op jit(solution)/shard_map/ppermute | solution.py:35
  384.0 19.1 %collective-permute-start.77 = (f32[128,2,128]{0,2,1:T(8,128)S(1)}, f32[128,2,128]{0,2,1:T(8,128)S(1)}, u32[]{:S(2)}, u32[]{:S(2)}) collective-permute-start(f32[128,2,128]{0,2,1:T(8,128)S(1)} %get-tuple-element.1307), channel_id=1, source_target_pairs={{0,8},{4,12},{8,16},{12,20},{16,24},{20,28},{24,32},{28,36},{32,40... | collective-permute-start | bytes 393224 | tf_op jit(solution)/shard_map/ppermute | solution.py:35
  (65 other events, 872.4 us)
where the time goes:
time: 521 us; the launch traced here: 517 us
  starting transfers between devices  281 us (54%)
  blocking collectives  122 us (23%)
  waiting for transfers between devices  39.2 us (8%)
  local copies, waits for them, and re-layouts  21.6 us (4%)
  matrix products  21.5 us (4%)
  between operations  17.8 us (3%)
  other arithmetic  13.2 us (3%)
    ppermute x80, starting transfers between devices, shifted(): return lax.ppermute(array, axis, pairs)  257 us
    psum x4, blocking collectives, over_axes(): array = lax.psum(array, axis)  70.7 us
    all_to_all x3, blocking collectives, from_everyone(): return lax.all_to_all(copies, axis, split_axis=0, concat_axis=0, tiled=True)  27.2 us
    all_to_all x2, blocking collectives, summed_on_arrival(): lax.all_to_all(parts, axis, split_axis=0, concat_axis=0, tiled=True)  24.5 us
    ppermute x80, waiting for transfers between devices, shifted(): return lax.ppermute(array, axis, pairs)  22.4 us
    all_to_all x2, starting transfers between devices, from_everyone(): return lax.all_to_all(copies, axis, split_axis=0, concat_axis=0, tiled=True)  14.1 us
    all_to_all x2, waiting for transfers between devices, summed_on_arrival(): lax.all_to_all(parts, axis, split_axis=0, concat_axis=0, tiled=True)  13.2 us
  transfers between devices with their start and end apart: 84, of which 10 were waited for; matrix products, arithmetic and copies ran while one was open for 2% of the time, Pallas kernels for 0%

commit v1 on v0

--- a/solution.py
+++ b/solution.py
@@ -4,6 +4,7 @@
 from jax import lax
 from jax.sharding import Mesh
 from jax.sharding import PartitionSpec as P
+from jax.lax import all_gather
 
 HD = 128
 WIN = 1024
@@ -48,7 +49,7 @@
 
 def over_axes(array, axes):
     for axis in axes:
-        array = lax.psum(array, axis)
+        array = all_gather(array, axis_name=axis).sum(axis=0)
     return array
 
 

time: 521 us -> 577 us (1.11)
  the two profiles are of different devices: /device:TPU:2 before, /device:TPU:64 now
where the time goes in v1:
time: 577 us; the launch traced here: 573 us
  starting transfers between devices  266 us (46%)
  blocking collectives  167 us (29%)
  waiting for transfers between devices  55.3 us (10%)
  local copies, waits for them, and re-layouts  28 us (5%)
  matrix products  21.7 us (4%)
  between operations  20.2 us (4%)
  other arithmetic  14.5 us (3%)
    ppermute x80, starting transfers between devices, shifted(): return lax.ppermute(array, axis, pairs)  250 us
    all_gather x4, blocking collectives, over_axes(): array = all_gather(array, axis_name=axis).sum(axis=0)  71.6 us
    unnamed x4, blocking collectives  43.3 us
    ppermute x80, waiting for transfers between devices, shifted(): return lax.ppermute(array, axis, pairs)  42.3 us
    all_to_all x3, blocking collectives, from_everyone(): return lax.all_to_all(copies, axis, split_axis=0, concat_axis=0, tiled=True)  27.2 us
    all_to_all x2, blocking collectives, summed_on_arrival(): lax.all_to_all(parts, axis, split_axis=0, concat_axis=0, tiled=True)  25 us
    unnamed x62, local copies, waits for them, and re-layouts  12.1 us
  transfers between devices with their start and end apart: 84, of which 13 were waited for; matrix products, arithmetic and copies ran while one was open for 3% of the time, Pallas kernels for 0%

profile of v1, /device:TPU:64, one launch (start us, length us, event | category | flops | bytes accessed | tf_op | source)
XLA Modules:
  0.0 572.9 jit_solution(3803015608392209092)
XLA Ops:
  18.4 4.5 collective-permute-start
  33.0 5.0 collective-permute-start.4
  54.3 4.7 collective-permute-start.10
  61.1 5.7 collective-permute-start.12
  75.9 5.2 collective-permute-done.15
  107.6 5.2 collective-permute-start.24
  129.8 4.6 collective-permute-start.31
  137.7 5.5 collective-permute-done.31
  144.8 4.8 all-to-all-start.2
  151.3 7.7 %all-to-all-done.2 = f32[4,128,256]{2,1,0:T(8,128)} async-done(((f32[4,128,256]{2,1,0:T(8,128)}), f32[4,128,256]{2,1,0:T(8,128)}, u32[]{:S(2)}, u32[]{:S(2)}) %all-to-all-start.2) | async-done | bytes 524320 | tf_op jit(solution)/shard_map/all_to_all | solution.py:46
  164.1 9.1 %all_to_all.45 = bf16[4,128,256]{1,2,0:T(8,128)(2,1)S(1)} all-to-all(bf16[4,128,256]{1,2,0:T(8,128)(2,1)S(1)} %broadcast_in_dim.55), channel_id=1, replica_groups=mesh['seq_0'=8,'seq_1'=8,'seq_2'=2,'tp'=4] {'tp'}, dimensions={0} | all-to-all | bytes 524288 | tf_op jit(solution)/shard_map/all_to_all | solution.py:19
  192.0 4.6 collective-permute-start.38
  196.6 5.5 collective-permute-start.39
  218.6 4.5 collective-permute-start.46
  230.5 5.9 %collective-permute-done.47 = f32[128,2,128]{0,2,1:T(8,128)S(1)} collective-permute-done((f32[128,2,128]{0,2,1:T(8,128)S(1)}, f32[128,2,128]{0,2,1:T(8,128)S(1)}, u32[]{:S(2)}, u32[]{:S(2)}) %collective-permute-start.47) | collective-permute-done | bytes 131104 | tf_op jit(solution)/shard_map/ppermute | solution.py:36
  237.1 12.4 %all_to_all.48 = f32[4,128,256]{2,1,0:T(8,128)} all-to-all(f32[4,128,256]{2,1,0:T(8,128)S(1)} %bitcast.206), channel_id=1, replica_groups=mesh['seq_0'=8,'seq_1'=8,'seq_2'=2,'tp'=4] {'tp'}, dimensions={0} | all-to-all | bytes 1048576 | tf_op jit(solution)/shard_map/all_to_all | solution.py:46
  254.0 9.1 %all_to_all.46 = bf16[4,128,256]{1,2,0:T(8,128)(2,1)S(1)} all-to-all(bf16[4,128,256]{1,2,0:T(8,128)(2,1)S(1)} %broadcast_in_dim.56), channel_id=1, replica_groups=mesh['seq_0'=8,'seq_1'=8,'seq_2'=2,'tp'=4] {'tp'}, dimensions={0} | all-to-all | bytes 524288 | tf_op jit(solution)/shard_map/all_to_all | solution.py:19
  281.8 4.6 collective-permute-start.54
  286.5 5.5 collective-permute-start.55
  312.9 4.4 collective-permute-start.63
  320.5 5.8 %collective-permute-done.63 = f32[128,2,128]{0,2,1:T(8,128)S(1)} collective-permute-done((f32[128,2,128]{0,2,1:T(8,128)S(1)}, f32[128,2,128]{0,2,1:T(8,128)S(1)}, u32[]{:S(2)}, u32[]{:S(2)}) %collective-permute-start.63) | collective-permute-done | bytes 131104 | tf_op jit(solution)/shard_map/ppermute | solution.py:36
  327.1 12.5 %all_to_all.49 = f32[4,128,256]{2,1,0:T(8,128)} all-to-all(f32[4,128,256]{2,1,0:T(8,128)S(1)} %bitcast.207), channel_id=1, replica_groups=mesh['seq_0'=8,'seq_1'=8,'seq_2'=2,'tp'=4] {'tp'}, dimensions={0} | all-to-all | bytes 1048576 | tf_op jit(solution)/shard_map/all_to_all | solution.py:46
  344.1 9.1 %all_to_all.47 = bf16[4,128,256]{1,2,0:T(8,128)(2,1)S(1)} all-to-all(bf16[4,128,256]{1,2,0:T(8,128)(2,1)S(1)} %broadcast_in_dim.57), channel_id=1, replica_groups=mesh['seq_0'=8,'seq_1'=8,'seq_2'=2,'tp'=4] {'tp'}, dimensions={0} | all-to-all | bytes 524288 | tf_op jit(solution)/shard_map/all_to_all | solution.py:19
  371.8 4.6 collective-permute-start.70
  376.5 5.5 collective-permute-start.71
  410.5 5.9 %collective-permute-done.79 = f32[128,2,128]{0,2,1:T(8,128)S(1)} collective-permute-done((f32[128,2,128]{0,2,1:T(8,128)S(1)}, f32[128,2,128]{0,2,1:T(8,128)S(1)}, u32[]{:S(2)}, u32[]{:S(2)}) %collective-permute-start.79) | collective-permute-done | bytes 131104 | tf_op jit(solution)/shard_map/ppermute | solution.py:36
  434.1 38.4 %all-gather.8 = f32[8,4,4]{2,1,0:T(4,128)S(1)} all-gather(f32[1,4,4]{2,1,0:T(4,128)S(1)} %convolution_bitcast_fusion.9), channel_id=6, replica_groups=mesh['seq_0'=8,'seq_1'=8,'seq_2'=2,'tp'=4] {'seq_0'}, dimensions={0}, use_global_device_ids=true | all-gather | bytes 576 | tf_op jit(solution)/shard_map/all_gather | solution.py:52
  472.5 20.8 %all-gather.9 = f32[8,4,4]{2,1,0:T(4,128)S(1)} all-gather(f32[1,4,4]{2,1,0:T(4,128)S(1)} %bitcast.251), channel_id=7, replica_groups=mesh['seq_0'=8,'seq_1'=8,'seq_2'=2,'tp'=4] {'seq_1'}, dimensions={0}, use_global_device_ids=true | all-gather | bytes 576 | tf_op jit(solution)/shard_map/all_gather | solution.py:52
  495.2 10.6 %all-gather.11 = f32[4,4,4]{2,1,0:T(4,128)S(1)} all-gather(f32[1,4,4]{2,1,0:T(4,128)S(1)} %bitcast.253), channel_id=9, replica_groups=mesh['seq_0'=8,'seq_1'=8,'seq_2'=2,'tp'=4] {'tp'}, dimensions={0}, use_global_device_ids=true | all-gather | bytes 320 | tf_op jit(solution)/shard_map/all_gather | solution.py:52
  510.3 16.1 %all-reduce = f32[32]{0:T(128)S(1)} all-reduce(f32[32]{0:T(128)S(1)} %dynamic-update-slice.131), channel_id=2, replica_groups=mesh['seq_0'=8,'seq_1'=8,'seq_2'=2,'tp'=4] {'seq_0'}, use_global_device_ids=true, to_apply=%add | all-reduce | flops 32 | bytes 256
  526.7 15.3 %all-reduce.1 = f32[32]{0:T(128)S(1)} all-reduce(f32[32]{0:T(128)S(1)} %dynamic-update-slice.132), channel_id=3, replica_groups=mesh['seq_0'=8,'seq_1'=8,'seq_2'=2,'tp'=4] {'seq_1'}, use_global_device_ids=true, to_apply=%add.1 | all-reduce | flops 32 | bytes 256
  545.8 9.5 %all-reduce.3 = f32[16]{0:T(128)S(1)} all-reduce(f32[16]{0:T(128)S(1)} %dynamic-update-slice.134), channel_id=5, replica_groups=mesh['seq_0'=8,'seq_1'=8,'seq_2'=2,'tp'=4] {'tp'}, use_global_device_ids=true, to_apply=%add.3 | all-reduce | flops 16 | bytes 128
  (323 shorter events, 280.0 us)
Async XLA Ops:
  14.2 23.8 %all-to-all-start.1 = ((bf16[4,128,256]{1,2,0:T(8,128)(2,1)}), bf16[4,128,256]{1,2,0:T(8,128)(2,1)S(1)}, u32[]{:S(2)}, u32[]{:S(2)}) async-start(bf16[4,128,256]{1,2,0:T(8,128)(2,1)} %broadcast_in_dim.54), calls=%async_computation.1 | async-start | bytes 524288 | tf_op jit(solution)/shard_map/all_to_all | solution.py:19
  18.4 20.8 %collective-permute-start = (bf16[128,2,128]{2,0,1:T(8,128)(2,1)S(1)}, bf16[128,2,128]{2,0,1:T(8,128)(2,1)S(1)}, u32[]{:S(2)}, u32[]{:S(2)}) collective-permute-start(bf16[128,2,128]{2,0,1:T(8,128)(2,1)S(1)} %bitcast.243), channel_id=1, source_target_pairs={{0,16},{4,20},{8,24},{12,28},{16,32},{20,36},{24,40},{28,44},{32,4... | collective-permute-start | bytes 196616 | tf_op jit(solution)/shard_map/ppermute | solution.py:36
  22.9 18.6 %collective-permute-start.1 = (bf16[128,2,128]{2,0,1:T(8,128)(2,1)S(1)}, bf16[128,2,128]{2,0,1:T(8,128)(2,1)S(1)}, u32[]{:S(2)}, u32[]{:S(2)}) collective-permute-start(bf16[128,2,128]{2,0,1:T(8,128)(2,1)S(1)} %bitcast.244), channel_id=1, source_target_pairs={{0,12},{4,16},{8,20},{12,24},{16,28},{20,32},{24,36},{28,40},{32,4... | collective-permute-start | bytes 196616 | tf_op jit(solution)/shard_map/ppermute | solution.py:36
  24.8 18.6 %collective-permute-start.2 = (bf16[128,2,128]{2,0,1:T(8,128)(2,1)S(1)}, bf16[128,2,128]{2,0,1:T(8,128)(2,1)}, u32[]{:S(2)}, u32[]{:S(2)}) collective-permute-start(bf16[128,2,128]{2,0,1:T(8,128)(2,1)S(1)} %bitcast.245), channel_id=1, source_target_pairs={{0,8},{4,12},{8,16},{12,20},{16,24},{20,28},{24,32},{28,36},{32,40... | collective-permute-start | bytes 196616 | tf_op jit(solution)/shard_map/ppermute | solution.py:36
  28.9 17.9 %collective-permute-start.3 = (bf16[128,2,128]{2,0,1:T(8,128)(2,1)S(1)}, bf16[128,2,128]{2,0,1:T(8,128)(2,1)S(1)}, u32[]{:S(2)}, u32[]{:S(2)}) collective-permute-start(bf16[128,2,128]{2,0,1:T(8,128)(2,1)S(1)} %bitcast.246), channel_id=1, source_target_pairs={{0,4},{4,8},{8,12},{12,16},{16,20},{20,24},{24,28},{28,32},{32,36}... | collective-permute-start | bytes 196616 | tf_op jit(solution)/shard_map/ppermute | solution.py:36
  33.0 18.2 %collective-permute-start.4 = (bf16[128,2,128]{2,0,1:T(8,128)(2,1)S(1)}, bf16[128,2,128]{2,0,1:T(8,128)(2,1)S(1)}, u32[]{:S(2)}, u32[]{:S(2)}) collective-permute-start(bf16[128,2,128]{2,0,1:T(8,128)(2,1)S(1)} %bitcast.247), channel_id=1, source_target_pairs={{4,0},{8,4},{12,8},{16,12},{20,16},{24,20},{28,24},{32,28},{36,32}... | collective-permute-start | bytes 196616 | tf_op jit(solution)/shard_map/ppermute | solution.py:36
  41.5 17.5 %collective-permute-start.6 = (bf16[128,2,128]{2,0,1:T(8,128)(2,1)S(1)}, bf16[128,2,128]{2,0,1:T(8,128)(2,1)S(1)}, u32[]{:S(2)}, u32[]{:S(2)}) collective-permute-start(bf16[128,2,128]{2,0,1:T(8,128)(2,1)S(1)} %bitcast.249), channel_id=1, source_target_pairs={{12,0},{16,4},{20,8},{24,12},{28,16},{32,20},{36,24},{40,28},{44,3... | collective-permute-start | bytes 196616 | tf_op jit(solution)/shard_map/ppermute | solution.py:36
  43.5 17.6 %collective-permute-start.7 = (bf16[128,2,128]{2,0,1:T(8,128)(2,1)S(1)}, bf16[128,2,128]{2,0,1:T(8,128)(2,1)S(1)}, u32[]{:S(2)}, u32[]{:S(2)}) collective-permute-start(bf16[128,2,128]{2,0,1:T(8,128)(2,1)S(1)} %bitcast.250), channel_id=1, source_target_pairs={{16,0},{20,4},{24,8},{28,12},{32,16},{36,20},{40,24},{44,28},{48,3... | collective-permute-start | bytes 196616 | tf_op jit(solution)/shard_map/ppermute | solution.py:36
  46.7 21.1 %collective-permute-start.8 = (bf16[128,2,128]{2,0,1:T(8,128)(2,1)}, bf16[128,2,128]{2,0,1:T(8,128)(2,1)S(1)}, u32[]{:S(2)}, u32[]{:S(2)}) collective-permute-start(bf16[128,2,128]{2,0,1:T(8,128)(2,1)} %bitcast.198), channel_id=1, source_target_pairs={{0,16},{4,20},{8,24},{12,28},{16,32},{20,36},{24,40},{28,44},{32,4... | collective-permute-start | bytes 196616 | tf_op jit(solution)/shard_map/ppermute | solution.py:36
  51.2 18.7 %collective-permute-start.9 = (bf16[128,2,128]{2,0,1:T(8,128)(2,1)}, bf16[128,2,128]{2,0,1:T(8,128)(2,1)S(1)}, u32[]{:S(2)}, u32[]{:S(2)}) collective-permute-start(bf16[128,2,128]{2,0,1:T(8,128)(2,1)} %bitcast.198), channel_id=1, source_target_pairs={{0,12},{4,16},{8,20},{12,24},{16,28},{20,32},{24,36},{28,40},{32,4... | collective-permute-start | bytes 196616 | tf_op jit(solution)/shard_map/ppermute | solution.py:36
  54.3 17.5 %collective-permute-start.10 = (bf16[128,2,128]{2,0,1:T(8,128)(2,1)}, bf16[128,2,128]{2,0,1:T(8,128)(2,1)S(1)}, u32[]{:S(2)}, u32[]{:S(2)}) collective-permute-start(bf16[128,2,128]{2,0,1:T(8,128)(2,1)} %bitcast.198), channel_id=1, source_target_pairs={{0,8},{4,12},{8,16},{12,20},{16,24},{20,28},{24,32},{28,36},{32,40... | collective-permute-start | bytes 196616 | tf_op jit(solution)/shard_map/ppermute | solution.py:36
  93.2 19.6 %collective-permute-start.20 = (f32[128,2,128]{0,2,1:T(8,128)S(1)}, f32[128,2,128]{0,2,1:T(8,128)S(1)}, u32[]{:S(2)}, u32[]{:S(2)}) collective-permute-start(f32[128,2,128]{0,2,1:T(8,128)S(1)} %get-tuple-element.1340), channel_id=1, source_target_pairs={{0,4},{4,8},{8,12},{12,16},{16,20},{20,24},{24,28},{28,32},{32,36}... | collective-permute-start | bytes 393224 | tf_op jit(solution)/shard_map/ppermute | solution.py:36
  95.6 19.6 %collective-permute-start.21 = (f32[128,2,128]{0,2,1:T(8,128)S(1)}, f32[128,2,128]{0,2,1:T(8,128)S(1)}, u32[]{:S(2)}, u32[]{:S(2)}) collective-permute-start(f32[128,2,128]{0,2,1:T(8,128)S(1)} %get-tuple-element.1339), channel_id=1, source_target_pairs={{0,8},{4,12},{8,16},{12,20},{16,24},{20,28},{24,32},{28,36},{32,40... | collective-permute-start | bytes 393224 | tf_op jit(solution)/shard_map/ppermute | solution.py:36
  99.3 18.3 %collective-permute-start.22 = (f32[128,2,128]{0,2,1:T(8,128)S(1)}, f32[128,2,128]{0,2,1:T(8,128)S(1)}, u32[]{:S(2)}, u32[]{:S(2)}) collective-permute-start(f32[128,2,128]{0,2,1:T(8,128)S(1)} %get-tuple-element.1338), channel_id=1, source_target_pairs={{0,12},{4,16},{8,20},{12,24},{16,28},{20,32},{24,36},{28,40},{32,4... | collective-permute-start | bytes 393224 | tf_op jit(solution)/shard_map/ppermute | solution.py:36
  103.7 16.4 %collective-permute-start.23 = (f32[128,2,128]{0,2,1:T(8,128)S(1)}, f32[128,2,128]{0,2,1:T(8,128)S(1)}, u32[]{:S(2)}, u32[]{:S(2)}) collective-permute-start(f32[128,2,128]{0,2,1:T(8,128)S(1)} %get-tuple-element.1337), channel_id=1, source_target_pairs={{0,16},{4,20},{8,24},{12,28},{16,32},{20,36},{24,40},{28,44},{32,4... | collective-permute-start | bytes 393224 | tf_op jit(solution)/shard_map/ppermute | solution.py:36
  117.6 16.9 %collective-permute-start.27 = (f32[128,2,128]{0,2,1:T(8,128)S(1)}, f32[128,2,128]{0,2,1:T(8,128)S(1)}, u32[]{:S(2)}, u32[]{:S(2)}) collective-permute-start(f32[128,2,128]{0,2,1:T(8,128)S(1)} %get-tuple-element.1349), channel_id=1, source_target_pairs={{16,0},{20,4},{24,8},{28,12},{32,16},{36,20},{40,24},{44,28},{48,3... | collective-permute-start | bytes 393224 | tf_op jit(solution)/shard_map/ppermute | solution.py:36
  184.1 17.9 %collective-permute-start.35 = (f32[128,2,128]{0,2,1:T(8,128)S(1)}, f32[128,2,128]{0,2,1:T(8,128)S(1)}, u32[]{:S(2)}, u32[]{:S(2)}) collective-permute-start(f32[128,2,128]{0,2,1:T(8,128)S(1)} %get-tuple-element.1325), channel_id=1, source_target_pairs={{16,0},{20,4},{24,8},{28,12},{32,16},{36,20},{40,24},{44,28},{48,3... | collective-permute-start | bytes 393224 | tf_op jit(solution)/shard_map/ppermute | solution.py:36
  186.2 20.0 %collective-permute-start.36 = (f32[128,2,128]{0,2,1:T(8,128)S(1)}, f32[128,2,128]{0,2,1:T(8,128)S(1)}, u32[]{:S(2)}, u32[]{:S(2)}) collective-permute-start(f32[128,2,128]{0,2,1:T(8,128)S(1)} %get-tuple-element.1324), channel_id=1, source_target_pairs={{0,4},{4,8},{8,12},{12,16},{16,20},{20,24},{24,28},{28,32},{32,36}... | collective-permute-start | bytes 393224 | tf_op jit(solution)/shard_map/ppermute | solution.py:36
  188.6 19.8 %collective-permute-start.37 = (f32[128,2,128]{0,2,1:T(8,128)S(1)}, f32[128,2,128]{0,2,1:T(8,128)S(1)}, u32[]{:S(2)}, u32[]{:S(2)}) collective-permute-start(f32[128,2,128]{0,2,1:T(8,128)S(1)} %get-tuple-element.1323), channel_id=1, source_target_pairs={{0,8},{4,12},{8,16},{12,20},{16,24},{20,28},{24,32},{28,36},{32,40... | collective-permute-start | bytes 393224 | tf_op jit(solution)/shard_map/ppermute | solution.py:36
  192.0 18.7 %collective-permute-start.38 = (f32[128,2,128]{0,2,1:T(8,128)S(1)}, f32[128,2,128]{0,2,1:T(8,128)S(1)}, u32[]{:S(2)}, u32[]{:S(2)}) collective-permute-start(f32[128,2,128]{0,2,1:T(8,128)S(1)} %get-tuple-element.1322), channel_id=1, source_target_pairs={{0,12},{4,16},{8,20},{12,24},{16,28},{20,32},{24,36},{28,40},{32,4... | collective-permute-start | bytes 393224 | tf_op jit(solution)/shard_map/ppermute | solution.py:36
  196.6 16.5 %collective-permute-start.39 = (f32[128,2,128]{0,2,1:T(8,128)S(1)}, f32[128,2,128]{0,2,1:T(8,128)S(1)}, u32[]{:S(2)}, u32[]{:S(2)}) collective-permute-start(f32[128,2,128]{0,2,1:T(8,128)S(1)} %get-tuple-element.1321), channel_id=1, source_target_pairs={{0,16},{4,20},{8,24},{12,28},{16,32},{20,36},{24,40},{28,44},{32,4... | collective-permute-start | bytes 393224 | tf_op jit(solution)/shard_map/ppermute | solution.py:36
  210.7 16.9 %collective-permute-start.43 = (f32[128,2,128]{0,2,1:T(8,128)S(1)}, f32[128,2,128]{0,2,1:T(8,128)S(1)}, u32[]{:S(2)}, u32[]{:S(2)}) collective-permute-start(f32[128,2,128]{0,2,1:T(8,128)S(1)} %get-tuple-element.1333), channel_id=1, source_target_pairs={{16,0},{20,4},{24,8},{28,12},{32,16},{36,20},{40,24},{44,28},{48,3... | collective-permute-start | bytes 393224 | tf_op jit(solution)/shard_map/ppermute | solution.py:36
  274.0 18.0 %collective-permute-start.51 = (f32[128,2,128]{0,2,1:T(8,128)S(1)}, f32[128,2,128]{0,2,1:T(8,128)S(1)}, u32[]{:S(2)}, u32[]{:S(2)}) collective-permute-start(f32[128,2,128]{0,2,1:T(8,128)S(1)} %get-tuple-element.1309), channel_id=1, source_target_pairs={{16,0},{20,4},{24,8},{28,12},{32,16},{36,20},{40,24},{44,28},{48,3... | collective-permute-start | bytes 393224 | tf_op jit(solution)/shard_map/ppermute | solution.py:36
  275.9 20.1 %collective-permute-start.52 = (f32[128,2,128]{0,2,1:T(8,128)S(1)}, f32[128,2,128]{0,2,1:T(8,128)S(1)}, u32[]{:S(2)}, u32[]{:S(2)}) collective-permute-start(f32[128,2,128]{0,2,1:T(8,128)S(1)} %get-tuple-element.1308), channel_id=1, source_target_pairs={{0,4},{4,8},{8,12},{12,16},{16,20},{20,24},{24,28},{28,32},{32,36}... | collective-permute-start | bytes 393224 | tf_op jit(solution)/shard_map/ppermute | solution.py:36
  278.4 19.9 %collective-permute-start.53 = (f32[128,2,128]{0,2,1:T(8,128)S(1)}, f32[128,2,128]{0,2,1:T(8,128)S(1)}, u32[]{:S(2)}, u32[]{:S(2)}) collective-permute-start(f32[128,2,128]{0,2,1:T(8,128)S(1)} %get-tuple-element.1307), channel_id=1, source_target_pairs={{0,8},{4,12},{8,16},{12,20},{16,24},{20,28},{24,32},{28,36},{32,40... | collective-permute-start | bytes 393224 | tf_op jit(solution)/shard_map/ppermute | solution.py:36
  281.8 18.8 %collective-permute-start.54 = (f32[128,2,128]{0,2,1:T(8,128)S(1)}, f32[128,2,128]{0,2,1:T(8,128)S(1)}, u32[]{:S(2)}, u32[]{:S(2)}) collective-permute-start(f32[128,2,128]{0,2,1:T(8,128)S(1)} %get-tuple-element.1306), channel_id=1, source_target_pairs={{0,12},{4,16},{8,20},{12,24},{16,28},{20,32},{24,36},{28,40},{32,4... | collective-permute-start | bytes 393224 | tf_op jit(solution)/shard_map/ppermute | solution.py:36
  300.6 16.9 %collective-permute-start.59 = (f32[128,2,128]{0,2,1:T(8,128)S(1)}, f32[128,2,128]{0,2,1:T(8,128)S(1)}, u32[]{:S(2)}, u32[]{:S(2)}) collective-permute-start(f32[128,2,128]{0,2,1:T(8,128)S(1)} %get-tuple-element.1317), channel_id=1, source_target_pairs={{16,0},{20,4},{24,8},{28,12},{32,16},{36,20},{40,24},{44,28},{48,3... | collective-permute-start | bytes 393224 | tf_op jit(solution)/shard_map/ppermute | solution.py:36
  364.0 18.0 %collective-permute-start.67 = (f32[128,2,128]{0,2,1:T(8,128)S(1)}, f32[128,2,128]{0,2,1:T(8,128)S(1)}, u32[]{:S(2)}, u32[]{:S(2)}) collective-permute-start(f32[128,2,128]{0,2,1:T(8,128)S(1)} %get-tuple-element.1293), channel_id=1, source_target_pairs={{16,0},{20,4},{24,8},{28,12},{32,16},{36,20},{40,24},{44,28},{48,3... | collective-permute-start | bytes 393224 | tf_op jit(solution)/shard_map/ppermute | solution.py:36
  366.0 20.1 %collective-permute-start.68 = (f32[128,2,128]{0,2,1:T(8,128)S(1)}, f32[128,2,128]{0,2,1:T(8,128)S(1)}, u32[]{:S(2)}, u32[]{:S(2)}) collective-permute-start(f32[128,2,128]{0,2,1:T(8,128)S(1)} %get-tuple-element.1292), channel_id=1, source_target_pairs={{0,4},{4,8},{8,12},{12,16},{16,20},{20,24},{24,28},{28,32},{32,36}... | collective-permute-start | bytes 393224 | tf_op jit(solution)/shard_map/ppermute | solution.py:36
  368.4 19.9 %collective-permute-start.69 = (f32[128,2,128]{0,2,1:T(8,128)S(1)}, f32[128,2,128]{0,2,1:T(8,128)S(1)}, u32[]{:S(2)}, u32[]{:S(2)}) collective-permute-start(f32[128,2,128]{0,2,1:T(8,128)S(1)} %get-tuple-element.1291), channel_id=1, source_target_pairs={{0,8},{4,12},{8,16},{12,20},{16,24},{20,28},{24,32},{28,36},{32,40... | collective-permute-start | bytes 393224 | tf_op jit(solution)/shard_map/ppermute | solution.py:36
  371.8 18.8 %collective-permute-start.70 = (f32[128,2,128]{0,2,1:T(8,128)S(1)}, f32[128,2,128]{0,2,1:T(8,128)S(1)}, u32[]{:S(2)}, u32[]{:S(2)}) collective-permute-start(f32[128,2,128]{0,2,1:T(8,128)S(1)} %get-tuple-element.1290), channel_id=1, source_target_pairs={{0,12},{4,16},{8,20},{12,24},{16,28},{20,32},{24,36},{28,40},{32,4... | collective-permute-start | bytes 393224 | tf_op jit(solution)/shard_map/ppermute | solution.py:36
  390.6 16.9 %collective-permute-start.75 = (f32[128,2,128]{0,2,1:T(8,128)S(1)}, f32[128,2,128]{0,2,1:T(8,128)S(1)}, u32[]{:S(2)}, u32[]{:S(2)}) collective-permute-start(f32[128,2,128]{0,2,1:T(8,128)S(1)} %get-tuple-element.1301), channel_id=1, source_target_pairs={{16,0},{20,4},{24,8},{28,12},{32,16},{36,20},{40,24},{44,28},{48,3... | collective-permute-start | bytes 393224 | tf_op jit(solution)/shard_map/ppermute | solution.py:36
  (65 other events, 951.8 us)
